TPU v7x, 32 devices: a whole 2x2x4 slice. The times are simulated.
32 devices in a mesh: ia: 4 (over y, x), ja: 8 (over z, core).
Axes of the slice: x: 2, y: 2, z: 4, core: 2. Of those that a mesh axis runs over, the one named last changes fastest.
Arguments:
- phase_space: float32 [12, 8192], P(None, 'ja'), may hold values from -6 to 6
- star_mass: float32 [8192], P('ja'), may hold values from 6.1035156e-05 to 0.00024414062
- star_level: int32 [8192], P('ja'), may hold values from 0 to 3
- active_ids: int32 [2, 64, 128], P(None, 'ia'), may hold values from 0 to 8191, as said below
- active_counts: int32 [2, 64], P(None, 'ia'), may hold values from 1 to 128, as said below
Outputs:
- final_state: float32 [12, 8192], P(None, 'ja')
- active_force: float32 [2, 6, 8192], P(None, None, ('ia', 'ja'))
Inputs may be any that keep to these rules, and one draw needn't show every extreme that they name: `active_ids`: within one block step the 64 x 128 entries are distinct star numbers; entries of unused slots are ignored. `active_counts`: in every block step one block is full and one holds a single star.
All inputs are finite; a program needn't handle non-finite values.
Results may differ from a plain program's by a relative error of at most 0.00018.
Values sent between devices are 32-bit elements; how exact they have to be, the bound alone decides.
A program may use at most 64 MiB of HBM per device.

v0:
```python
import jax
import jax.numpy as jnp
from jax import lax
from jax.sharding import PartitionSpec as P

STEPS = 2


EPS2 = 0.01
STEP_TIME = 0.05


def predict(state, tau):
    tau_sq = tau * tau
    tau_cube = tau_sq * tau
    new_pos = (
        state[0:3] + state[3:6] * tau + state[6:9] * (tau_sq * 0.5) + state[9:12] * (tau_cube / 6.0)
    )
    new_vel = state[3:6] + state[6:9] * tau + state[9:12] * (tau_sq * 0.5)
    return (new_pos, new_vel)


def field_force(target_pos, target_vel, source_pos, source_vel, source_mass):
    offset = source_pos[:, None, :] - target_pos[:, :, None]
    rel_vel = source_vel[:, None, :] - target_vel[:, :, None]
    dist_sq = jnp.sum(offset * offset, axis=0) + EPS2
    inverse = lax.rsqrt(dist_sq)
    weight = source_mass[None, :] * inverse * inverse * inverse
    radial = 3.0 * jnp.sum(offset * rel_vel, axis=0) / dist_sq
    accel = jnp.sum(weight[None] * offset, axis=2)
    jolt = jnp.sum(weight[None] * (rel_vel - radial[None] * offset), axis=2)
    return jnp.concatenate([accel, jolt], axis=0)


def blocked_force(target_pos, target_vel, source_pos, source_vel, source_mass, block_rows):
    total_rows = target_pos.shape[1]
    block_count = total_rows // block_rows
    tiles = (
        target_pos.reshape(3, block_count, block_rows).transpose(1, 0, 2),
        target_vel.reshape(3, block_count, block_rows).transpose(1, 0, 2),
    )

    def one_tile(pair_tile):
        return field_force(pair_tile[0], pair_tile[1], source_pos, source_vel, source_mass)

    result = lax.map(one_tile, tiles)
    return result.transpose(1, 0, 2).reshape(6, total_rows)


def correct(active_rows, accel, jolt, span):
    half_step = span * 0.5
    twelfth = span * span / 12.0
    old_pos = active_rows[0:3]
    old_vel = active_rows[3:6]
    old_acc = active_rows[6:9]
    old_jerk = active_rows[9:12]
    new_vel = old_vel + (old_acc + accel) * half_step + (old_jerk - jolt) * twelfth
    new_pos = old_pos + (old_vel + new_vel) * half_step + (old_acc - accel) * twelfth
    return jnp.concatenate([new_pos, new_vel, accel, jolt], axis=0)


def local(phase_space, star_mass, star_level, active_ids, active_counts):
    shard_width = phase_space.shape[1]
    shard_start = lax.axis_index("ja") * shard_width
    block_rows = 512
    state = phase_space
    last = -STEP_TIME * star_level.astype(jnp.float32)
    force_steps = []
    for step_index in range(STEPS):
        clock = STEP_TIME * (step_index + 1)
        indices = active_ids[step_index].reshape(-1)
        slot_pos = lax.broadcasted_iota(jnp.int32, (active_ids.shape[1], active_ids.shape[2]), 1)
        usable = (slot_pos < active_counts[step_index][:, None]).reshape(-1)
        local_ids = indices - shard_start
        inside = (local_ids >= 0) & (local_ids < shard_width)
        clipped = jnp.clip(local_ids, 0, shard_width - 1)
        fpos, fvel = predict(state, clock - last)
        stacked = jnp.concatenate([state, last[None, :]], axis=0)
        picked = jnp.where(inside[None, :], jnp.take(stacked, clipped, axis=1), 0.0)
        target_state = lax.psum(picked, "ja")
        tpos, tvel = predict(target_state[0:12], clock - target_state[12])
        partial_value = blocked_force(tpos, tvel, fpos, fvel, star_mass, block_rows)
        write_ids = jnp.where(usable, indices, -1)
        forces = lax.psum(partial_value, "ja")
        share_len = forces.shape[1] // lax.axis_size("ja")
        share_start = lax.axis_index("ja") * share_len
        force_share = lax.dynamic_slice_in_dim(forces, share_start, share_len, 1)
        usable_share = lax.dynamic_slice_in_dim(usable, share_start, share_len, 0)
        force_steps.append(jnp.where(usable_share[None, :], force_share, 0.0))
        outgoing = correct(target_state[0:12], forces[0:3], forces[3:6], clock - target_state[12])
        returned, return_ids = (
            lax.all_gather(outgoing, "ia", axis=1, tiled=True),
            lax.all_gather(write_ids, "ia", axis=0, tiled=True),
        )
        placed_raw = return_ids - shard_start
        valid = (return_ids >= 0) & (placed_raw >= 0) & (placed_raw < shard_width)
        placed = jnp.where(valid, placed_raw, shard_width)
        state = state.at[:, placed].set(returned, mode="drop")
        last = last.at[placed].set(clock, mode="drop")
    return (state, jnp.stack(force_steps))


def solution(mesh):
    placed = (P(None, "ja"), P("ja"), P("ja"), P(None, "ia", None), P(None, "ia"))
    return jax.shard_map(
        local,
        mesh=mesh,
        in_specs=placed,
        out_specs=(P(None, "ja"), P(None, None, ("ia", "ja"))),
        check_vma=False,
    )
```

profile of v0, /device:TPU:0, one launch (start us, length us, event | category | flops | bytes accessed | tf_op | source)
XLA Modules:
  0.0 312.6 jit_solution(17012939076392843902)
XLA Ops:
  7.2 0.8 slice_bitcast_fusion
  8.0 0.7 convert_multiply_fusion
  8.7 0.9 pad_maximum_fusion.3
  9.5 0.2 copy.110
  9.7 0.7 compare_and_fusion.2
  10.5 0.8 fusion.19
  11.3 5.5 %gather_fusion = f32[2048,13]{1,0:T(8,128)S(1)} fusion(f32[13,1024]{0,1:T(8,128)S(1)} %copy.110, s32[2048]{0:T(1024)S(1)} %get-tuple-element.164), kind=kCustom, calls=%fused_computation.clone | custom fusion | bytes 221184 | tf_op jit(solution)/shard_map/jit(_take)/gather | solution.py:79
  16.7 0.3 copy.111
  17.1 0.7 bitcast_select_fusion.1
  17.9 9.6 %all_gather.14 = s32[8192]{0:T(1024)S(1)} all-gather(s32[2048]{0:T(1024)S(1)} %get-tuple-element.165), channel_id=1, replica_groups=mesh['ia'=4,'ja'=8] {'ia'}, dimensions={0}, use_global_device_ids=true | all-gather | bytes 40960 | tf_op jit(solution)/shard_map/all_gather | solution.py:93
  27.5 8.1 %all_gather.12 = s32[8192]{0:T(1024)S(1)} all-gather(s32[2048]{0:T(1024)S(1)} %get-tuple-element.166), channel_id=1, replica_groups=mesh['ia'=4,'ja'=8] {'ia'}, dimensions={0}, use_global_device_ids=true | all-gather | bytes 40960 | tf_op jit(solution)/shard_map/all_gather | solution.py:93
  35.7 30.4 %scatter_fusion.1 = f32[1024]{0:T(1024)S(1)} fusion(f32[1024]{0:T(1024)S(1)} %get-tuple-element.170, s32[8192]{0:T(1024)S(1)} %compare_select_fusion.1, f32[8192]{0:T(1024)S(1)} %broadcast.175), kind=kCustom, calls=%fused_computation.3 | custom fusion | bytes 131072 | tf_op jit(solution)/shard_map/scatter | solution.py:99
  66.3 0.2 copy.114
  66.7 0.2 copy.116
  66.9 7.9 %all-reduce.3.cloned.1.call-done = f32[13,2048]{1,0:T(8,128)} async-done(((f32[13,2048]{1,0:T(8,128)}), f32[13,2048]{1,0:T(8,128)}) %all-reduce.3.cloned.1.call-update) | async-done | bytes 106512 | tf_op jit(solution)/shard_map/psum | solution.py:80
  74.8 0.9 broadcast_multiply_fusion.1
  75.7 1.0 multiply_add_fusion.4
  76.8 20.9 %while.20 = (s32[]{:T(128)}, f32[4,6,512]{2,1,0:T(8,128)S(1)}, f32[1024]{0:T(1024)S(1)}, f32[3,1024]{1,0:T(4,128)S(1)}, f32[4,3,512]{2,1,0:T(4,128)S(1)}, /*inde...) while((s32[]{:T(128)}, f32[4,6,512]{2,1,0:T(8,128)S(1)}, f32[1024]{0:T(1024)S(1)}, ...), condition=%wide.region_6.8_spmd, body=%wide.region_1.7_spmd.sunk | while | flops 24117248 | bytes 16924772 | solution.py:46
  76.8 1.8 fusion.31
  78.6 0.9 multiply_divide_fusion.4
  79.5 2.4 fusion.32
  82.0 1.8 fusion.31
  83.8 0.9 multiply_divide_fusion.4
  84.8 2.4 fusion.32
  87.2 1.8 fusion.31
  89.0 0.9 multiply_divide_fusion.4
  90.0 2.4 fusion.32
  92.5 1.8 fusion.31
  94.3 0.9 multiply_divide_fusion.4
  95.2 2.4 fusion.32
  97.7 26.3 %psum.29 = f32[6,2048]{1,0:T(8,128)S(1)} all-reduce(f32[6,2048]{1,0:T(8,128)S(1)} %bitcast.106), channel_id=1, replica_groups=mesh['ia'=4,'ja'=8] {'ja'}, use_global_device_ids=true, to_apply=%region_7.9 | all-reduce | flops 12288 | bytes 98304 | tf_op jit(solution)/shard_map/psum | solution.py:84
  124.1 10.1 %all_gather.13 = f32[12,8192]{1,0:T(8,128)S(1)} all-gather(f32[12,2048]{1,0:T(8,128)S(1)} %pad_maximum_fusion.1), channel_id=1, replica_groups=mesh['ia'=4,'ja'=8] {'ia'}, dimensions={1}, use_global_device_ids=true | all-gather | bytes 491520 | tf_op jit(solution)/shard_map/all_gather | solution.py:92
  134.2 2.6 copy.115
  136.8 21.2 %scatter_fusion = f32[12,1024]{0,1:T(8,128)S(1)} fusion(f32[12,1024]{0,1:T(8,128)S(1)} %copy.114, s32[8192]{0:T(1024)S(1)} %compare_select_fusion.1, f32[8192,12]{1,0:T(8,128)} %copy.115), kind=kCustom, calls=%fused_computation.2 | custom fusion | bytes 1212416 | tf_op jit(solution)/shard_map/scatter | solution.py:98
  158.1 1.3 fusion.24
  159.3 0.2 pad_maximum_fusion
  159.5 7.6 %gather_fusion.1 = f32[2048,13]{1,0:T(8,128)} fusion(f32[13,1024]{0,1:T(8,128)S(1)} %pad_maximum_fusion, s32[2048]{0:T(1024)S(1)} %get-tuple-element.163), kind=kCustom, calls=%fused_computation.1.clone | custom fusion | bytes 221184 | tf_op jit(solution)/shard_map/jit(_take)/gather | solution.py:79
  167.1 1.5 copy.117
  168.7 0.7 bitcast_select_fusion
  169.4 1.2 copy.129
  170.8 0.2 copy.128
  171.0 0.2 copy.131
  171.3 50.0 %all-reduce.5.cloned.1.call-done = f32[13,2048]{1,0:T(8,128)} async-done(((f32[13,2048]{1,0:T(8,128)}), f32[13,2048]{1,0:T(8,128)}) %all-reduce.5.cloned.1.call-update) | async-done | bytes 106512 | tf_op jit(solution)/shard_map/psum | solution.py:80
  221.3 0.9 broadcast_multiply_fusion
  222.1 1.0 multiply_add_fusion.1
  223.2 20.9 %while.21 = (s32[]{:T(128)}, f32[4,6,512]{2,1,0:T(8,128)S(1)}, f32[1024]{0:T(1024)S(1)}, f32[3,1024]{1,0:T(4,128)S(1)}, f32[4,3,512]{2,1,0:T(4,128)S(1)}, /*inde...) while((s32[]{:T(128)}, f32[4,6,512]{2,1,0:T(8,128)S(1)}, f32[1024]{0:T(1024)S(1)}, ...), condition=%wide.region_16.18_spmd, body=%wide.region_11.17_spmd.sunk | while | flops 24117248 | bytes 16924772 | solution.py:46
  223.2 1.8 fusion.34
  225.0 0.9 multiply_divide_fusion.5
  226.0 2.4 fusion.35
  228.4 1.8 fusion.34
  230.2 0.9 multiply_divide_fusion.5
  231.2 2.4 fusion.35
  233.7 1.8 fusion.34
  235.5 0.9 multiply_divide_fusion.5
  236.4 2.4 fusion.35
  238.9 1.8 fusion.34
  240.7 0.9 multiply_divide_fusion.5
  241.7 2.4 fusion.35
  244.1 26.3 %psum.31 = f32[6,2048]{1,0:T(8,128)S(1)} all-reduce(f32[6,2048]{1,0:T(8,128)S(1)} %bitcast.105), channel_id=1, replica_groups=mesh['ia'=4,'ja'=8] {'ja'}, use_global_device_ids=true, to_apply=%region_17.19 | all-reduce | flops 12288 | bytes 98304 | tf_op jit(solution)/shard_map/psum | solution.py:84
  270.6 10.0 %all_gather.15 = f32[12,8192]{1,0:T(8,128)S(1)} all-gather(f32[12,2048]{1,0:T(8,128)S(1)} %pad_maximum_fusion.2), channel_id=1, replica_groups=mesh['ia'=4,'ja'=8] {'ia'}, dimensions={1}, use_global_device_ids=true | all-gather | bytes 491520 | tf_op jit(solution)/shard_map/all_gather | solution.py:92
  280.6 2.6 copy.124
  283.2 21.1 %scatter_fusion.2 = f32[12,1024]{0,1:T(8,128)S(1)} fusion(f32[12,1024]{0,1:T(8,128)S(1)} %scatter_fusion, s32[8192]{0:T(1024)S(1)} %compare_select_fusion, f32[8192,12]{1,0:T(8,128)} %copy.124), kind=kCustom, calls=%fused_computation.4 | custom fusion | bytes 1212416 | tf_op jit(solution)/shard_map/scatter | solution.py:98
  304.3 0.8 copy.127
  305.1 0.6 pad_maximum_fusion.4
  (49 shorter events, 1.1 us)
Async XLA Ops:
  7.2 67.6 %all-reduce.3.cloned.1.call-start = ((), (), s32[]{:S(2)}) async-start(), calls=%async_computation | async-start | bytes 262144 | tf_op jit(solution)/shard_map/psum | solution.py:80
  17.8 203.5 %all-reduce.5.cloned.1.call-start = ((), (), s32[]{:S(2)}) async-start(), calls=%async_computation.1 | async-start | bytes 262144 | tf_op jit(solution)/shard_map/psum | solution.py:80
  35.7 30.5 %copy-start = (f32[12,1024]{1,0:T(8,128)S(1)}, f32[12,1024]{1,0:T(8,128)}, u32[]{:S(2)}) copy-start(f32[12,1024]{1,0:T(8,128)} %param.11) | copy-start | bytes 147460
  35.7 41.0 %copy-start.3 = (f32[1024]{0:T(1024)S(1)}, f32[1024]{0:T(1024)}, u32[]{:S(2)}) copy-start(f32[1024]{0:T(1024)} %param.12) | copy-start | bytes 12292
  76.7 47.3 %copy-start.1 = (f32[13,2048]{1,0:T(8,128)S(1)}, f32[13,2048]{1,0:T(8,128)}, u32[]{:S(2)}) copy-start(f32[13,2048]{1,0:T(8,128)} %all-reduce.3.cloned.1.call-done) | copy-start | bytes 319492
  223.2 47.3 %copy-start.2 = (f32[13,2048]{1,0:T(8,128)S(1)}, f32[13,2048]{1,0:T(8,128)}, u32[]{:S(2)}) copy-start(f32[13,2048]{1,0:T(8,128)} %all-reduce.5.cloned.1.call-done) | copy-start | bytes 319492
Sparse Core Ops, SparseCore 0:
  17.9 56.8 all-reduce.2
  169.5 51.6 all-reduce.4
where the time goes:
time: 313 us
  local copies, waits for them, and re-layouts  98.5 us (31%)
  blocking collectives  90.5 us (29%)
  waiting for transfers between devices  57.9 us (18%)
  other arithmetic  50.9 us (16%)
  between operations  14.3 us (5%)
    psum x2, waiting for transfers between devices, local(): target_state = lax.psum(picked, 'ja')  57.9 us
    psum x2, blocking collectives, local(): forces = lax.psum(partial_value, 'ja')  52.7 us
    scatter x2, local copies, waits for them, and re-layouts, local(): state = state.at[:, placed].set(returned, mode='drop')  42.3 us
    scatter x1, local copies, waits for them, and re-layouts, local(): last = last.at[placed].set(clock, mode='drop')  30.4 us
    all_gather x2, blocking collectives, local(): lax.all_gather(outgoing, 'ia', axis=1, tiled=True)  20.1 us
    reduce_sum x8, other arithmetic, field_force(): accel = jnp.sum(weight[None] * offset, axis=2)  19.5 us
    all_gather x2, blocking collectives, local(): lax.all_gather(write_ids, 'ia', axis=0, tiled=True)  17.7 us
    gather x4, local copies, waits for them, and re-layouts, local(): picked = jnp.where(inside[None, :], jnp.take(stacked, clipped, axis=1), 0.0)  14.9 us
  transfers between devices with their start and end apart: 2, of which 2 were waited for; matrix products, arithmetic and copies ran while one was open for 11% of the time, Pallas kernels for 0%

commit v1 on v0

--- a/solution.py
+++ b/solution.py
@@ -1,6 +1,10 @@
+import functools
+
 import jax
 import jax.numpy as jnp
 from jax import lax
+from jax.experimental import pallas as pl
+from jax.experimental.pallas import tpu as pltpu
 from jax.sharding import PartitionSpec as P
 
 STEPS = 2
@@ -100,10 +104,315 @@
     return (state, jnp.stack(force_steps))
 
 
+MESH = pl.DeviceIdType.MESH
+TILE = 16
+VMEM = pl.BlockSpec(memory_space=pltpu.VMEM)
+
+
+def pieces(values):
+    high = values.astype(jnp.bfloat16)
+    rest = values - high.astype(jnp.float32)
+    middle = rest.astype(jnp.bfloat16)
+    low = (rest - middle.astype(jnp.float32)).astype(jnp.bfloat16)
+    return high, middle, low
+
+
+def pick(values, onehot, dims):
+    total = None
+    for piece in pieces(values):
+        term = lax.dot_general(piece, onehot, (dims, ((), ())), preferred_element_type=jnp.float32)
+        total = term if total is None else total + term
+    return total
+
+
+def peers(sizes):
+    num_i, num_j = sizes
+    me_i, me_j = lax.axis_index("ia"), lax.axis_index("ja")
+    along_j = [(me_i, lax.rem(me_j + step, num_j)) for step in range(1, num_j)]
+    along_i = [(lax.rem(me_i + step, num_i), me_j) for step in range(1, num_i)]
+    return along_j, along_i
+
+
+def greet(others):
+    barrier = pltpu.get_barrier_semaphore()
+    for other in others:
+        pl.semaphore_signal(barrier, inc=1, device_id=other, device_id_type=MESH)
+    pl.semaphore_wait(barrier, len(others))
+
+
+def send(source, target, send_sem, recv_sem, other):
+    copy = pltpu.make_async_remote_copy(
+        src_ref=source,
+        dst_ref=target,
+        send_sem=send_sem,
+        recv_sem=recv_sem,
+        device_id=other,
+        device_id_type=MESH,
+    )
+    copy.start()
+    return copy
+
+
+def spread(sizes, all_ref, along_j, along_i, sj, rj, si, ri):
+    me_i, me_j = lax.axis_index("ia"), lax.axis_index("ja")
+    mine = all_ref.at[me_i, me_j]
+    copies = [send(mine, mine, sj.at[n], rj.at[n], other) for n, other in enumerate(along_j)]
+    for copy in copies:
+        copy.wait()
+    column = all_ref.at[me_i]
+    return [send(column, column, si.at[n], ri.at[n], other) for n, other in enumerate(along_i)]
+
+
+def first_kernel(sizes, state_ref, mass_ref, level_ref, ids_ref, all_ref, ids_all_ref, own_ref, sj, rj, si, ri, sk, rk):
+    me_i, me_j = lax.axis_index("ia"), lax.axis_index("ja")
+    width = own_ref.shape[1]
+    part = pl.ds(pl.multiple_of(me_i * width, width), width)
+    along_j, along_i = peers(sizes)
+    greet(along_j + along_i)
+    ids_all_ref[me_i] = ids_ref[...]
+    named = ids_all_ref.at[me_i]
+    copies = [send(named, named, sk.at[n], rk.at[n], other) for n, other in enumerate(along_i)]
+    state = state_ref[:, part]
+    mass = mass_ref[:, part]
+    last = -STEP_TIME * level_ref[:, part].astype(jnp.float32)
+    pos, vel = predict(state, STEP_TIME - last)
+    all_ref[me_i, me_j, 0:3, :] = pos
+    all_ref[me_i, me_j, 3:6, :] = vel
+    all_ref[me_i, me_j, 6:8, :] = jnp.concatenate([mass, mass], axis=0)
+    own_ref[0:12, :] = state
+    own_ref[12:14, :] = jnp.concatenate([mass, last], axis=0)
+    own_ref[14:24, :] = jnp.zeros((10, width), jnp.float32)
+    copies += spread(sizes, all_ref, along_j, along_i, sj, rj, si, ri)
+    for copy in copies:
+        copy.wait()
+
+
+def second_kernel(sizes, block_ref, all_ref, sj, rj, si, ri):
+    me_i, me_j = lax.axis_index("ia"), lax.axis_index("ja")
+    along_j, along_i = peers(sizes)
+    greet(along_j + along_i)
+    all_ref[me_i, me_j] = block_ref[...]
+    for copy in spread(sizes, all_ref, along_j, along_i, sj, rj, si, ri):
+        copy.wait()
+
+
+def force_kernel(sizes, step_index, all_ref, ids_ref, own_ref, *refs):
+    if step_index == 0:
+        block_ref, new_ref, target_ref, total_ref = refs
+    else:
+        new_ref, target_ref, total_ref = refs
+    num_i, num_j = sizes
+    me_i, me_j = lax.axis_index("ia"), lax.axis_index("ja")
+    width = own_ref.shape[1]
+    lanes = 128
+    clock = STEP_TIME * (step_index + 1)
+    stars = (me_j * num_i + me_i) * width + lax.broadcasted_iota(jnp.int32, (width, lanes), 0)
+
+    def match(row, seen):
+        for inner in range(ids_ref.shape[3]):
+            seen = jnp.where(ids_ref[row // num_j, step_index, lax.rem(row, num_j), inner : inner + 1, :] == stars, 1.0, seen)
+        return seen
+
+    seen = lax.fori_loop(0, num_i * num_j, match, jnp.zeros((width, lanes), jnp.float32))
+    used_column = jnp.broadcast_to(jnp.max(seen, axis=1, keepdims=True), (width, lanes))
+    used = jnp.transpose(used_column)[0:8]
+    before = lax.broadcasted_iota(jnp.int32, (width, width), 0) < lax.broadcasted_iota(jnp.int32, (width, width), 1)
+    before = jnp.where(before, 1.0, 0.0).astype(jnp.bfloat16)
+    rank = jnp.dot(used.astype(jnp.bfloat16), before, preferred_element_type=jnp.float32)[0:1]
+    used = used[0:1]
+    wanted = jnp.where(used > 0.5, rank, -1.0).astype(jnp.int32)
+    onehot = jnp.where(lax.broadcasted_iota(jnp.int32, (width, width), 0) == wanted, 1.0, 0.0).astype(jnp.bfloat16)
+    count = jnp.sum(used).astype(jnp.int32)
+    targets = None
+    for piece in pieces(all_ref[me_i * num_j + me_j]):
+        term = lax.dot_general(onehot, piece, (((1,), (1,)), ((), ())), preferred_element_type=jnp.float32)
+        targets = term if targets is None else targets + term
+    for row in range(6):
+        target_ref[row] = jnp.broadcast_to(targets[:, row : row + 1], (width, lanes))
+    total_ref[...] = jnp.zeros_like(total_ref)
+
+    def tile(index, carry):
+        rows = pl.ds(pl.multiple_of(index * TILE, TILE), TILE)
+        tx, ty, tz, tu, tv, tw = [target_ref[row, rows, :] for row in range(6)]
+
+        def chunk(block, sums):
+            for first in range(0, width, lanes):
+                sx, sy, sz, su, sv, sw, mass = [
+                    all_ref[block, row : row + 1, first : first + lanes] for row in range(7)
+                ]
+                ax, ay, az, jx, jy, jz = sums
+                dx, dy, dz = sx - tx, sy - ty, sz - tz
+                wx, wy, wz = su - tu, sv - tv, sw - tw
+                inverse = lax.rsqrt((dx * dx + dy * dy + dz * dz) + EPS2)
+                square = inverse * inverse
+                weight = (mass * inverse) * square
+                radial = (dx * wx + dy * wy + dz * wz) * (3.0 * square)
+                sums = (
+                    ax + weight * dx,
+                    ay + weight * dy,
+                    az + weight * dz,
+                    jx + weight * (wx - radial * dx),
+                    jy + weight * (wy - radial * dy),
+                    jz + weight * (wz - radial * dz),
+                )
+            return sums
+
+        zero = jnp.zeros((TILE, lanes), jnp.float32)
+        sums = lax.fori_loop(0, num_i * num_j, chunk, (zero,) * 6)
+        for row in range(6):
+            total_ref[row, rows, :] = sums[row]
+        return carry
+
+    lax.fori_loop(0, (count + TILE - 1) // TILE, tile, 0)
+    lane = lax.broadcasted_iota(jnp.int32, (width, lanes), 1)
+    packed = jnp.zeros((width, lanes), jnp.float32)
+    for row in range(6):
+        packed = jnp.where(lane == row, jnp.sum(total_ref[row], axis=1, keepdims=True), packed)
+    force = pick(jnp.transpose(packed)[0:8], onehot, ((1,), (0,)))[0:6]
+    state = own_ref[0:12, :]
+    mass, last = own_ref[12:13, :], own_ref[13:14, :]
+    moved = correct(state, force[0:3], force[3:6], clock - last)
+    state = jnp.where(used > 0.5, moved, state)
+    new_ref[0:12, :] = state
+    if step_index == 0:
+        last = jnp.where(used > 0.5, clock, last)
+        new_ref[12:14, :] = jnp.concatenate([mass, last], axis=0)
+        new_ref[14:18, :] = jnp.zeros((4, width), jnp.float32)
+        new_ref[18:24, :] = force
+        pos, vel = predict(state, STEP_TIME * (step_index + 2) - last)
+        block_ref[0:3, :] = pos
+        block_ref[3:6, :] = vel
+        block_ref[6:8, :] = jnp.concatenate([mass, mass], axis=0)
+    else:
+        new_ref[12:18, :] = own_ref[18:24, :]
+        new_ref[18:24, :] = force
+
+
+def last_kernel(sizes, own_ref, ids_ref, state_ref, force_ref, rows_ref, part_ref, got_ref, si, ri, sj, rj):
+    num_i, num_j = sizes
+    me_i, me_j = lax.axis_index("ia"), lax.axis_index("ja")
+    width = own_ref.shape[1]
+    lanes = 128
+    along_j, along_i = peers(sizes)
+    greet(along_j + along_i)
+    rows_ref[me_i] = own_ref[...]
+    mine = rows_ref.at[me_i]
+    copies = [send(mine, mine, si.at[n], ri.at[n], other) for n, other in enumerate(along_i)]
+    for copy in copies:
+        copy.wait()
+    for block in range(num_i):
+        state_ref[:, block * width : (block + 1) * width] = rows_ref[block, 0:12, :]
+    star = me_j * (num_i * width) + lax.broadcasted_iota(jnp.int32, (num_i * width, lanes), 0)
+    tables = []
+    for step_index in range(STEPS):
+        table = jnp.concatenate(
+            [rows_ref[block, 12 + 6 * step_index : 18 + 6 * step_index, :] for block in range(num_i)], axis=1
+        )
+        table = jnp.concatenate([table, jnp.zeros((2, num_i * width), jnp.float32)], axis=0)
+        tables.append(pieces(table))
+
+    def share(owner, carry):
+        for step_index in range(STEPS):
+            for row in range(ids_ref.shape[2]):
+                names = ids_ref[step_index, owner, row : row + 1, :]
+                onehot = jnp.where(star == names, 1.0, 0.0).astype(jnp.bfloat16)
+                total = None
+                for piece in tables[step_index]:
+                    term = jnp.dot(piece, onehot, preferred_element_type=jnp.float32)
+                    total = term if total is None else total + term
+                part_ref[owner, step_index, :, row * lanes : (row + 1) * lanes] = total
+        return carry
+
+    lax.fori_loop(0, num_j, share, 0)
+    copies = [
+        send(part_ref.at[other[1]], got_ref.at[me_j], sj.at[n], rj.at[n], other) for n, other in enumerate(along_j)
+    ]
+    for copy in copies:
+        copy.wait()
+    total = part_ref[me_j]
+    for step in range(1, num_j):
+        total = total + got_ref[lax.rem(me_j + step, num_j)]
+    force_ref[...] = total[:, 0:6, :]
+
+
+def star_order(sizes, phase_space, star_mass, star_level, active_ids, active_counts):
+    num_i, num_j = sizes
+    shard = phase_space.shape[1]
+    width = shard // num_i
+    f32 = jnp.float32
+    rows, lanes = active_ids.shape[1], active_ids.shape[2]
+    slot_pos = lax.broadcasted_iota(jnp.int32, active_ids.shape, 2)
+    ids = jnp.where(slot_pos < active_counts[:, :, None], active_ids, -1)
+    ids = ids.reshape(STEPS, num_j, rows // num_j, lanes)
+    dma_j, dma_i = pltpu.SemaphoreType.DMA((num_j - 1,)), pltpu.SemaphoreType.DMA((num_i - 1,))
+    whole = jax.ShapeDtypeStruct((num_i, num_j, 8, width), f32)
+    own_shape = jax.ShapeDtypeStruct((24, width), f32)
+
+    def remote(number):
+        return pltpu.CompilerParams(collective_id=number, has_side_effects=True, vmem_limit_bytes=32 * 2**20)
+
+    local_params = pltpu.CompilerParams(vmem_limit_bytes=32 * 2**20)
+    every, ids_all, own = pl.pallas_call(
+        functools.partial(first_kernel, sizes),
+        out_shape=(whole, jax.ShapeDtypeStruct((num_i,) + ids.shape, jnp.int32), own_shape),
+        in_specs=[VMEM] * 4,
+        out_specs=(VMEM,) * 3,
+        scratch_shapes=[dma_j, dma_j, dma_i, dma_i, dma_i, dma_i],
+        compiler_params=remote(0),
+    )(phase_space, star_mass.reshape(1, shard), star_level.reshape(1, shard), ids)
+    work = [pltpu.VMEM((6, width, 128), f32), pltpu.VMEM((6, width, 128), f32)]
+    block, own = pl.pallas_call(
+        functools.partial(force_kernel, sizes, 0),
+        out_shape=(jax.ShapeDtypeStruct((8, width), f32), own_shape),
+        in_specs=[VMEM] * 3,
+        out_specs=(VMEM,) * 2,
+        scratch_shapes=work,
+        compiler_params=local_params,
+    )(every.reshape(num_i * num_j, 8, width), ids_all, own)
+    every = pl.pallas_call(
+        functools.partial(second_kernel, sizes),
+        out_shape=whole,
+        in_specs=[VMEM],
+        out_specs=VMEM,
+        scratch_shapes=[dma_j, dma_j, dma_i, dma_i],
+        compiler_params=remote(1),
+    )(block)
+    own = pl.pallas_call(
+        functools.partial(force_kernel, sizes, 1),
+        out_shape=own_shape,
+        in_specs=[VMEM] * 3,
+        out_specs=VMEM,
+        scratch_shapes=work,
+        compiler_params=local_params,
+    )(every.reshape(num_i * num_j, 8, width), ids_all, own)
+    share = (rows // num_j) * lanes
+    parts = pltpu.VMEM((num_j, STEPS, 8, share), f32)
+    return pl.pallas_call(
+        functools.partial(last_kernel, sizes),
+        out_shape=(
+            jax.ShapeDtypeStruct((12, shard), f32),
+            jax.ShapeDtypeStruct((STEPS, 6, share), f32),
+        ),
+        in_specs=[VMEM] * 2,
+        out_specs=(VMEM,) * 2,
+        scratch_shapes=[pltpu.VMEM((num_i, 24, width), f32), parts, parts, dma_i, dma_i, dma_j, dma_j],
+        compiler_params=remote(2),
+    )(own, ids)
+
+
 def solution(mesh):
+    sizes = (mesh.shape["ia"], mesh.shape["ja"])
     placed = (P(None, "ja"), P("ja"), P("ja"), P(None, "ia", None), P(None, "ia"))
+
+    def chosen(phase_space, star_mass, star_level, active_ids, active_counts):
+        stars = phase_space.shape[1] * sizes[1]
+        slots = active_ids.shape[1] * active_ids.shape[2] * sizes[0]
+        if stars == slots:
+            return star_order(sizes, phase_space, star_mass, star_level, active_ids, active_counts)
+        return local(phase_space, star_mass, star_level, active_ids, active_counts)
+
     return jax.shard_map(
-        local,
+        chosen,
         mesh=mesh,
         in_specs=placed,
         out_specs=(P(None, "ja"), P(None, None, ("ia", "ja"))),

time: 313 us -> 64.2 us (0.21)
  local copies, waits for them, and re-layouts: 98.5 us -> 2.75 us
  blocking collectives: 90.5 us -> 0 us
  Pallas kernels: 0 us -> 59.7 us
  waiting for transfers between devices: 57.9 us -> 0 us
  other arithmetic: 50.9 us -> 0.81 us
  between operations: 14.3 us -> 0.69 us
    scatter x3 -> x0, local copies, waits for them, and re-layouts: 72.7 us -> none  [the longest x2 42.3 us: local(): state = state.at[:, placed].set(returned, mode='drop')]
    pallas_call x0 -> x5, Pallas kernels: none -> 59.7 us  [the longest x1 14.6 us: star_order(): pl.pallas_call(functools.partial(last_kernel, sizes), out_shape=(jax.Shap...]
    psum x2 -> x0, waiting for transfers between devices: 57.9 us -> none  [local(): target_state = lax.psum(picked, 'ja')]
    psum x2 -> x0, blocking collectives: 52.7 us -> none  [local(): forces = lax.psum(partial_value, 'ja')]
    all_gather x4 -> x0, blocking collectives: 37.8 us -> none  [the longest x2 20.1 us: local(): lax.all_gather(outgoing, 'ia', axis=1, tiled=True)]
    reduce_sum x16 -> x0, other arithmetic: 33.8 us -> none  [the longest x8 19.5 us: field_force(): accel = jnp.sum(weight[None] * offset, axis=2)]
    gather x4 -> x0, local copies, waits for them, and re-layouts: 14.9 us -> none  [local(): picked = jnp.where(inside[None, :], jnp.take(stacked, clipped, axis=1), 0.0)]
    div x8 -> x0, other arithmetic: 7.51 us -> none  [field_force(): radial = 3.0 * jnp.sum(offset * rel_vel, axis=0) / dist_sq]
  transfers between devices with their start and end apart: 2 -> 0, of which waited for: 2 -> 0; matrix products, arithmetic and copies ran while one was open for 11% -> 0% of each run, Pallas kernels for 0% -> 0%
where the time goes in v1:
time: 64.2 us; the launch traced here: 64 us
  Pallas kernels  59.7 us (93%)
  local copies, waits for them, and re-layouts  2.75 us (4%)
  other arithmetic  0.81 us (1%)
  between operations  0.69 us (1%)
    pallas_call x1, Pallas kernels, star_order(): pl.pallas_call(functools.partial(last_kernel, sizes), out_shape=(jax.Shap...  14.6 us
    pallas_call x1, Pallas kernels, star_order(): pl.pallas_call(functools.partial(first_kernel, sizes), out_shape=(whole,...  13.7 us
    pallas_call x1, Pallas kernels, star_order(): pl.pallas_call(functools.partial(second_kernel, sizes), out_shape=whole,...  12.8 us
    pallas_call x1, Pallas kernels, star_order(): pl.pallas_call(functools.partial(force_kernel, sizes, 1), out_shape=own_s...  9.75 us
    pallas_call x1, Pallas kernels, star_order(): pl.pallas_call(functools.partial(force_kernel, sizes, 0), out_shape=(jax....  8.84 us
    unnamed x9, local copies, waits for them, and re-layouts  2.14 us

profile of v1, /device:TPU:0, one launch (start us, length us, event | category | flops | bytes accessed | tf_op | source)
XLA Modules:
  0.0 64.0 jit_solution(17770685883565301157)
XLA Ops:
  0.6 0.0 copy-start.3
  0.6 0.7 %copy-done.3 = s32[2,16]{1,0:T(2,128)S(1)} copy-done((s32[2,16]{1,0:T(2,128)S(1)}, s32[2,16]{1,0:T(2,128)}, u32[]{:S(2)}) %copy-start.3) | copy-done | bytes 152
  1.3 0.0 copy-start.1
  1.3 0.0 copy-start.2
  1.3 0.8 %fusion = s32[2,16,128]{2,1,0:T(8,128)S(1)} fusion(s32[2,16,128]{2,1,0:T(8,128)} %param.8, s32[2,16]{1,0:T(2,128)S(1)} %copy-done.3), kind=kLoop, calls=%fused_computation.1 | loop fusion | flops 8192 | bytes 32896 | tf_op jit(solution)/shard_map/jit(_where)/select_n | solution.py:345
  2.1 0.0 copy-done.1
  2.1 0.0 copy-done.2
  2.1 0.0 copy-start
  2.2 0.8 %copy-done = f32[12,1024]{1,0:T(8,128)S(1)} copy-done((f32[12,1024]{1,0:T(8,128)S(1)}, f32[12,1024]{1,0:T(8,128)}, u32[]{:S(2)}) %copy-start) | copy-done | bytes 49176
  3.0 13.7 %shard_map.68 = (f32[4,8,8,256]{3,2,1,0:T(8,128)S(1)}, s32[4,2,8,2,128]{4,3,2,1,0:T(2,128)S(1)}, f32[24,256]{1,0:T(8,128)S(1)}) custom-call(f32[12,1024]{1,0:T(8,128)S(1)} %copy-done, f32[1,1024]{1,0:T(1,128)S(1)} %bitcast.9, s32[1,1024]{1,0:T(1,128)S(1)} %bitcast.10, s32[2,8,2,128]{3,2,1,0:T(2,128)S(1)} %bitcast.7), custom_call_target="tpu_custom_call" | custom-call | tf_op jit(solution)/shard_map/pallas_call | solution.py:355
  16.7 8.8 %shard_map.69 = (f32[8,256]{1,0:T(8,128)S(1)}, f32[24,256]{1,0:T(8,128)S(1)}) custom-call(f32[32,8,256]{2,1,0:T(8,128)S(1)} %bitcast.6, s32[4,2,8,2,128]{4,3,2,1,0:T(2,128)S(1)} %get-tuple-element.8.ids_ref, f32[24,256]{1,0:T(8,128)S(1)} %get-tuple-element.9.own_ref), custom_call_target="tpu_custom_call" | custom-call | tf_op jit(solution)/shard_map/pallas_call | solution.py:364
  25.6 12.8 %shard_map.70 = f32[4,8,8,256]{3,2,1,0:T(8,128)S(1)} custom-call(f32[8,256]{1,0:T(8,128)S(1)} %get-tuple-element.10.block_ref), custom_call_target="tpu_custom_call" | custom-call | tf_op jit(solution)/shard_map/pallas_call | solution.py:372
  38.4 9.7 %shard_map.71.own_ref = f32[24,256]{1,0:T(8,128)S(1)} custom-call(f32[32,8,256]{2,1,0:T(8,128)S(1)} %bitcast.5, s32[4,2,8,2,128]{4,3,2,1,0:T(2,128)S(1)} %get-tuple-element.8.ids_ref, f32[24,256]{1,0:T(8,128)S(1)} %get-tuple-element.11.own_ref), custom_call_target="tpu_custom_call" | custom-call | tf_op jit(solution)/shard_map/pallas_call | solution.py:380
  48.1 14.6 %shard_map.72 = (f32[12,1024]{1,0:T(8,128)S(1)}, f32[2,6,256]{2,1,0:T(8,128)S(1)}) custom-call(f32[24,256]{1,0:T(8,128)S(1)} %shard_map.71.own_ref, s32[2,8,2,128]{3,2,1,0:T(2,128)S(1)} %bitcast.8), custom_call_target="tpu_custom_call" | custom-call | tf_op jit(solution)/shard_map/pallas_call | solution.py:390
  62.8 0.6 copy.7
  63.4 0.6 copy.9
Async XLA Ops:
  0.6 0.7 %copy-start.3 = (s32[2,16]{1,0:T(2,128)S(1)}, s32[2,16]{1,0:T(2,128)}, u32[]{:S(2)}) copy-start(s32[2,16]{1,0:T(2,128)} %param.9) | copy-start | bytes 388
  1.3 0.8 %copy-start.1 = (f32[1024]{0:T(1024)S(1)}, f32[1024]{0:T(1024)}, u32[]{:S(2)}) copy-start(f32[1024]{0:T(1024)} %param.6) | copy-start | bytes 12292
  1.3 0.8 %copy-start.2 = (s32[1024]{0:T(1024)S(1)}, s32[1024]{0:T(1024)}, u32[]{:S(2)}) copy-start(s32[1024]{0:T(1024)} %param.7) | copy-start | bytes 12292
  2.1 0.8 %copy-start = (f32[12,1024]{1,0:T(8,128)S(1)}, f32[12,1024]{1,0:T(8,128)}, u32[]{:S(2)}) copy-start(f32[12,1024]{1,0:T(8,128)} %state_ref.1) | copy-start | bytes 147460

commit v2 on v0

--- a/solution.py
+++ b/solution.py
@@ -1,6 +1,10 @@
+import functools
+
 import jax
 import jax.numpy as jnp
 from jax import lax
+from jax.experimental import pallas as pl
+from jax.experimental.pallas import tpu as pltpu
 from jax.sharding import PartitionSpec as P
 
 STEPS = 2
@@ -100,10 +104,264 @@
     return (state, jnp.stack(force_steps))
 
 
+MESH = pl.DeviceIdType.MESH
+TILE = 16
+VMEM = pl.BlockSpec(memory_space=pltpu.VMEM)
+
+
+def pieces(values):
+    high = values.astype(jnp.bfloat16)
+    rest = values - high.astype(jnp.float32)
+    middle = rest.astype(jnp.bfloat16)
+    low = (rest - middle.astype(jnp.float32)).astype(jnp.bfloat16)
+    return high, middle, low
+
+
+def peers(sizes):
+    num_i, num_j = sizes
+    me_i, me_j = lax.axis_index("ia"), lax.axis_index("ja")
+    chips, chip, core = num_j // 2, me_j // 2, lax.rem(me_j, 2)
+    steps = sorted(range(chips), key=lambda step: min(step, chips - step))
+    along_j = []
+    for step in steps:
+        for flip in (0, 1):
+            if step or flip:
+                side = lax.rem(core + flip, 2)
+                ahead = lax.rem(chip + step, chips) * 2 + side
+                behind = lax.rem(chip + chips - step, chips) * 2 + side
+                along_j.append(((me_i, ahead), behind))
+    along_i = [((lax.rem(me_i + step, num_i), me_j), lax.rem(me_i + num_i - step, num_i)) for step in range(1, num_i)]
+    return along_j, along_i
+
+
+def send(source, target, send_sem, recv_sem, other):
+    copy = pltpu.make_async_remote_copy(
+        src_ref=source,
+        dst_ref=target,
+        send_sem=send_sem,
+        recv_sem=recv_sem,
+        device_id=other,
+        device_id_type=MESH,
+    )
+    copy.start()
+    return copy
+
+
+def whole_kernel(
+    sizes, state_ref, mass_ref, level_ref, ids_ref, out_ref, force_ref,
+    ids_all, field, field_next, rows_a, rows_b, part, got, target_ref, total_ref,
+    sk, rk, sf, rf, sg, rg, sa, ra, sb, rb, sp, rp, sq, rq,
+):
+    num_i, num_j = sizes
+    me_i, me_j = lax.axis_index("ia"), lax.axis_index("ja")
+    width, lanes = rows_a.shape[2], 128
+    along_j, along_i = peers(sizes)
+    own = pl.ds(pl.multiple_of(me_i * width, width), width)
+
+    def to_column(named, ssem, rsem):
+        return [send(named, named, ssem.at[n], rsem.at[n], other) for n, (other, _) in enumerate(along_i)]
+
+    def to_row(named, ssem, rsem):
+        return [send(named, named, ssem.at[n], rsem.at[n], other) for n, (other, _) in enumerate(along_j)]
+
+    def used_row(step_index):
+        stars = (me_j * num_i + me_i) * width + lax.broadcasted_iota(jnp.int32, (width, lanes), 0)
+
+        def match(row, seen):
+            for inner in range(ids_ref.shape[2]):
+                names = ids_all[row // num_j, step_index, lax.rem(row, num_j), inner : inner + 1, :]
+                seen = jnp.where(names == stars, 1.0, seen)
+            return seen
+
+        seen = lax.fori_loop(0, num_i * num_j, match, jnp.zeros((width, lanes), jnp.float32))
+        column = jnp.broadcast_to(jnp.max(seen, axis=1, keepdims=True), (width, lanes))
+        return jnp.transpose(column)[0:1] > 0.5
+
+    def set_targets(rows):
+        rows = jnp.concatenate([rows, jnp.zeros((lanes - 8, width), jnp.float32)], axis=0)
+        columns = jnp.transpose(rows)
+        for row in range(6):
+            target_ref[row] = jnp.broadcast_to(columns[:, row : row + 1], (width, lanes))
+        total_ref[...] = jnp.zeros_like(total_ref)
+
+    def accumulate(source, owner):
+        def tile(index, carry):
+            rows = pl.ds(pl.multiple_of(index * TILE, TILE), TILE)
+            tx, ty, tz, tu, tv, tw = [target_ref[row, rows, :] for row in range(6)]
+
+            def chunk(block, sums):
+                for first in range(0, width, lanes):
+                    sx, sy, sz, su, sv, sw, mass = [
+                        source[owner, block, row : row + 1, first : first + lanes] for row in range(7)
+                    ]
+                    ax, ay, az, jx, jy, jz = sums
+                    dx, dy, dz = sx - tx, sy - ty, sz - tz
+                    wx, wy, wz = su - tu, sv - tv, sw - tw
+                    inverse = lax.rsqrt((dx * dx + dy * dy + dz * dz) + EPS2)
+                    square = inverse * inverse
+                    weight = (mass * inverse) * square
+                    radial = (dx * wx + dy * wy + dz * wz) * (3.0 * square)
+                    sums = (
+                        ax + weight * dx,
+                        ay + weight * dy,
+                        az + weight * dz,
+                        jx + weight * (wx - radial * dx),
+                        jy + weight * (wy - radial * dy),
+                        jz + weight * (wz - radial * dz),
+                    )
+                return sums
+
+            sums = lax.fori_loop(0, num_i, chunk, tuple(total_ref[row, rows, :] for row in range(6)))
+            for row in range(6):
+                total_ref[row, rows, :] = sums[row]
+            return carry
+
+        lax.fori_loop(0, width // TILE, tile, 0)
+
+    def totals():
+        lane = lax.broadcasted_iota(jnp.int32, (width, lanes), 1)
+        packed = jnp.zeros((width, lanes), jnp.float32)
+        for row in range(6):
+            packed = jnp.where(lane == row, jnp.sum(total_ref[row], axis=1, keepdims=True), packed)
+        return jnp.transpose(packed)[0:6]
+
+    def share(step_index, blocks):
+        star = me_j * (num_i * width) + lax.broadcasted_iota(jnp.int32, (num_i * width, lanes), 0)
+        table = pieces(jnp.concatenate(blocks, axis=1))
+        tall = jnp.concatenate(table, axis=0)
+
+        def fill(owner, carry):
+            for row in range(ids_ref.shape[2]):
+                names = ids_ref[step_index, owner, row : row + 1, :]
+                onehot = jnp.where(star == names, 1.0, 0.0).astype(jnp.bfloat16)
+                found = jnp.dot(tall, onehot, preferred_element_type=jnp.float32)
+                part[step_index, owner, :, row * lanes : (row + 1) * lanes] = found[0:8] + found[8:16] + found[16:24]
+            return carry
+
+        lax.fori_loop(0, num_j, fill, 0)
+
+    def send_parts(step_index, ssem, rsem):
+        return [
+            send(part.at[step_index, other[1]], got.at[step_index, me_j], ssem.at[n], rsem.at[n], other)
+            for n, (other, _) in enumerate(along_j)
+        ]
+
+    greeting = [other for other, _ in along_j + along_i]
+    barrier = pltpu.get_barrier_semaphore()
+    for other in greeting:
+        pl.semaphore_signal(barrier, inc=1, device_id=other, device_id_type=MESH)
+    ids_all[me_i] = ids_ref[...]
+    mass_all = mass_ref[...]
+    pos, vel = predict(state_ref[...], STEP_TIME + STEP_TIME * level_ref[...].astype(jnp.float32))
+    for block in range(num_i):
+        some = slice(block * width, (block + 1) * width)
+        field[me_j, block] = jnp.concatenate([pos[:, some], vel[:, some], mass_all[:, some], mass_all[:, some]], axis=0)
+    pl.semaphore_wait(barrier, len(greeting))
+    loose = to_column(ids_all.at[me_i], sk, rk)
+    coming = to_row(field.at[me_j], sf, rf)
+    set_targets(field[me_j, me_i])
+    accumulate(field, me_j)
+    for copy in loose:
+        copy.wait()
+    used = used_row(0)
+    for copy, (_, owner) in zip(coming, along_j):
+        copy.wait_recv()
+        accumulate(field, owner)
+    for copy in coming:
+        copy.wait_send()
+    force = totals()
+    state = state_ref[:, own]
+    last = -STEP_TIME * level_ref[:, own].astype(jnp.float32)
+    state = jnp.where(used, correct(state, force[0:3], force[3:6], STEP_TIME - last), state)
+    last = jnp.where(used, STEP_TIME, last)
+    span = 2 * STEP_TIME - last
+    pos, vel = predict(state, span)
+    mass = mass_ref[:, own]
+    field_next[me_j, me_i] = jnp.concatenate([pos, vel, mass, mass], axis=0)
+    blank = jnp.zeros((2, width), jnp.float32)
+    rows_a[me_i] = jnp.concatenate([force, blank], axis=0)
+    column = to_column(field_next.at[me_j, me_i], sa, ra)
+    column_force = to_column(rows_a.at[me_i], sp, rp)
+    set_targets(field_next[me_j, me_i])
+    used = used_row(1)
+    for copy in column:
+        copy.wait()
+    coming = to_row(field_next.at[me_j], sg, rg)
+    accumulate(field_next, me_j)
+    for copy in column_force:
+        copy.wait()
+    share(0, [rows_a[block] for block in range(num_i)])
+    for copy, (_, owner) in zip(coming, along_j):
+        copy.wait_recv()
+        accumulate(field_next, owner)
+    for copy in coming:
+        copy.wait_send()
+    force = totals()
+    state = jnp.where(used, correct(state, force[0:3], force[3:6], span), state)
+    rows_b[me_i] = jnp.concatenate([force, blank[:, :], state, blank, blank], axis=0)
+    column = to_column(rows_b.at[me_i], sb, rb)
+    first_parts = send_parts(0, sq.at[0], rq.at[0])
+    for copy in column:
+        copy.wait()
+    share(1, [rows_b[block, 0:8, :] for block in range(num_i)])
+    second_parts = send_parts(1, sq.at[1], rq.at[1])
+    for block in range(num_i):
+        out_ref[:, block * width : (block + 1) * width] = rows_b[block, 8:20, :]
+    for step_index, parts in enumerate((first_parts, second_parts)):
+        for copy in parts:
+            copy.wait()
+        total = part[step_index, me_j]
+        for _, owner in along_j:
+            total = total + got[step_index, owner]
+        force_ref[step_index] = total[0:6]
+
+
+def star_order(sizes, phase_space, star_mass, star_level, active_ids, active_counts):
+    num_i, num_j = sizes
+    shard = phase_space.shape[1]
+    width = shard // num_i
+    f32 = jnp.float32
+    rows, lanes = active_ids.shape[1], active_ids.shape[2]
+    slot_pos = lax.broadcasted_iota(jnp.int32, active_ids.shape, 2)
+    ids = jnp.where(slot_pos < active_counts[:, :, None], active_ids, -1)
+    ids = ids.reshape(STEPS, num_j, rows // num_j, lanes)
+    share = (rows // num_j) * lanes
+    dma_j, dma_i = pltpu.SemaphoreType.DMA((num_j - 1,)), pltpu.SemaphoreType.DMA((num_i - 1,))
+    dma_2 = pltpu.SemaphoreType.DMA((STEPS, num_j - 1))
+    return pl.pallas_call(
+        functools.partial(whole_kernel, sizes),
+        out_shape=(jax.ShapeDtypeStruct((12, shard), f32), jax.ShapeDtypeStruct((STEPS, 6, share), f32)),
+        in_specs=[VMEM] * 4,
+        out_specs=(VMEM,) * 2,
+        scratch_shapes=[
+            pltpu.VMEM((num_i,) + ids.shape, jnp.int32),
+            pltpu.VMEM((num_j, num_i, 8, width), f32),
+            pltpu.VMEM((num_j, num_i, 8, width), f32),
+            pltpu.VMEM((num_i, 8, width), f32),
+            pltpu.VMEM((num_i, 24, width), f32),
+            pltpu.VMEM((STEPS, num_j, 8, share), f32),
+            pltpu.VMEM((STEPS, num_j, 8, share), f32),
+            pltpu.VMEM((6, width, 128), f32),
+            pltpu.VMEM((6, width, 128), f32),
+            dma_i, dma_i, dma_j, dma_j, dma_j, dma_j, dma_i, dma_i, dma_i, dma_i, dma_i, dma_i, dma_2, dma_2,
+        ],
+        compiler_params=pltpu.CompilerParams(collective_id=0, has_side_effects=True, vmem_limit_bytes=32 * 2**20),
+    )(phase_space, star_mass.reshape(1, shard), star_level.reshape(1, shard), ids)
+
+
 def solution(mesh):
+    sizes = (mesh.shape["ia"], mesh.shape["ja"])
     placed = (P(None, "ja"), P("ja"), P("ja"), P(None, "ia", None), P(None, "ia"))
+
+    def chosen(phase_space, star_mass, star_level, active_ids, active_counts):
+        stars = phase_space.shape[1] * sizes[1]
+        slots = active_ids.shape[1] * active_ids.shape[2] * sizes[0]
+        if stars == slots:
+            return star_order(sizes, phase_space, star_mass, star_level, active_ids, active_counts)
+        return local(phase_space, star_mass, star_level, active_ids, active_counts)
+
     return jax.shard_map(
-        local,
+        chosen,
         mesh=mesh,
         in_specs=placed,
         out_specs=(P(None, "ja"), P(None, None, ("ia", "ja"))),

time: 313 us -> 61 us (0.19)
  local copies, waits for them, and re-layouts: 98.5 us -> 2.75 us
  blocking collectives: 90.5 us -> 0 us
  waiting for transfers between devices: 57.9 us -> 0 us
  Pallas kernels: 0 us -> 56.5 us
  other arithmetic: 50.9 us -> 0.81 us
  between operations: 14.3 us -> 0.66 us
    scatter x3 -> x0, local copies, waits for them, and re-layouts: 72.7 us -> none  [the longest x2 42.3 us: local(): state = state.at[:, placed].set(returned, mode='drop')]
    psum x2 -> x0, waiting for transfers between devices: 57.9 us -> none  [local(): target_state = lax.psum(picked, 'ja')]
    pallas_call x0 -> x1, Pallas kernels: none -> 56.5 us  [star_order(): pl.pallas_call(functools.partial(whole_kernel, sizes), out_shape=(jax.Sha...]
    psum x2 -> x0, blocking collectives: 52.7 us -> none  [local(): forces = lax.psum(partial_value, 'ja')]
    all_gather x4 -> x0, blocking collectives: 37.8 us -> none  [the longest x2 20.1 us: local(): lax.all_gather(outgoing, 'ia', axis=1, tiled=True)]
    reduce_sum x16 -> x0, other arithmetic: 33.8 us -> none  [the longest x8 19.5 us: field_force(): accel = jnp.sum(weight[None] * offset, axis=2)]
    gather x4 -> x0, local copies, waits for them, and re-layouts: 14.9 us -> none  [local(): picked = jnp.where(inside[None, :], jnp.take(stacked, clipped, axis=1), 0.0)]
    div x8 -> x0, other arithmetic: 7.51 us -> none  [field_force(): radial = 3.0 * jnp.sum(offset * rel_vel, axis=0) / dist_sq]
  transfers between devices with their start and end apart: 2 -> 0, of which waited for: 2 -> 0; matrix products, arithmetic and copies ran while one was open for 11% -> 0% of each run, Pallas kernels for 0% -> 0%
where the time goes in v2:
time: 61 us; the launch traced here: 60.7 us
  Pallas kernels  56.5 us (93%)
  local copies, waits for them, and re-layouts  2.75 us (5%)
  other arithmetic  0.81 us (1%)
  between operations  0.66 us (1%)
    pallas_call x1, Pallas kernels, star_order(): pl.pallas_call(functools.partial(whole_kernel, sizes), out_shape=(jax.Sha...  56.5 us
    unnamed x9, local copies, waits for them, and re-layouts  2.14 us

profile of v2, /device:TPU:0, one launch (start us, length us, event | category | flops | bytes accessed | tf_op | source)
XLA Modules:
  0.0 60.7 jit_solution(7067435676706556030)
XLA Ops:
  0.6 0.0 copy-start.3
  0.6 0.7 %copy-done.3 = s32[2,16]{1,0:T(2,128)S(1)} copy-done((s32[2,16]{1,0:T(2,128)S(1)}, s32[2,16]{1,0:T(2,128)}, u32[]{:S(2)}) %copy-start.3) | copy-done | bytes 152
  1.3 0.0 copy-start.1
  1.3 0.0 copy-start.2
  1.3 0.8 %fusion = s32[2,16,128]{2,1,0:T(8,128)S(1)} fusion(s32[2,16,128]{2,1,0:T(8,128)} %param.8, s32[2,16]{1,0:T(2,128)S(1)} %copy-done.3), kind=kLoop, calls=%fused_computation.1 | loop fusion | flops 8192 | bytes 32896 | tf_op jit(solution)/shard_map/jit(_where)/select_n | solution.py:326
  2.1 0.0 copy-done.1
  2.1 0.0 copy-done.2
  2.1 0.0 copy-start
  2.2 0.8 %copy-done = f32[12,1024]{1,0:T(8,128)S(1)} copy-done((f32[12,1024]{1,0:T(8,128)S(1)}, f32[12,1024]{1,0:T(8,128)}, u32[]{:S(2)}) %copy-start) | copy-done | bytes 49176
  3.0 56.5 %shard_map.68 = (f32[12,1024]{1,0:T(8,128)S(1)}, f32[2,6,256]{2,1,0:T(8,128)S(1)}) custom-call(f32[12,1024]{1,0:T(8,128)S(1)} %copy-done, f32[1,1024]{1,0:T(1,128)S(1)} %bitcast.4, s32[1,1024]{1,0:T(1,128)S(1)} %bitcast.5, s32[2,8,2,128]{3,2,1,0:T(2,128)S(1)} %bitcast.3), custom_call_target="tpu_custom_call" | custom-call | tf_op jit(solution)/shard_map/pallas_call | solution.py:331
  59.5 0.6 copy.7
  60.1 0.6 %copy.9 = f32[12,1024]{1,0:T(8,128)} copy(f32[12,1024]{1,0:T(8,128)S(1)} %get-tuple-element.6) | data formatting | bytes 98304
Async XLA Ops:
  0.6 0.7 %copy-start.3 = (s32[2,16]{1,0:T(2,128)S(1)}, s32[2,16]{1,0:T(2,128)}, u32[]{:S(2)}) copy-start(s32[2,16]{1,0:T(2,128)} %param.9) | copy-start | bytes 388
  1.3 0.8 %copy-start.1 = (f32[1024]{0:T(1024)S(1)}, f32[1024]{0:T(1024)}, u32[]{:S(2)}) copy-start(f32[1024]{0:T(1024)} %param.6) | copy-start | bytes 12292
  1.3 0.8 %copy-start.2 = (s32[1024]{0:T(1024)S(1)}, s32[1024]{0:T(1024)}, u32[]{:S(2)}) copy-start(s32[1024]{0:T(1024)} %param.7) | copy-start | bytes 12292
  2.1 0.8 %copy-start = (f32[12,1024]{1,0:T(8,128)S(1)}, f32[12,1024]{1,0:T(8,128)}, u32[]{:S(2)}) copy-start(f32[12,1024]{1,0:T(8,128)} %state_ref.1) | copy-start | bytes 147460

commit v3 on v2

--- a/solution.py
+++ b/solution.py
@@ -148,9 +148,9 @@
 
 
 def whole_kernel(
-    sizes, state_ref, mass_ref, level_ref, ids_ref, out_ref, force_ref,
-    ids_all, field, field_next, rows_a, rows_b, part, got, target_ref, total_ref,
-    sk, rk, sf, rf, sg, rg, sa, ra, sb, rb, sp, rp, sq, rq,
+    sizes, state_in, mass_ref, level_ref, raw_ref, counts_ref, out_ref, force_ref,
+    state_ref, ids_all, field, field_next, rows_a, rows_b, part, got, target_ref, total_ref,
+    load_sem, sk, rk, sf, rf, sg, rg, sa, ra, sb, rb, sp, rp, sq, rq,
 ):
     num_i, num_j = sizes
     me_i, me_j = lax.axis_index("ia"), lax.axis_index("ja")
@@ -168,7 +168,7 @@
         stars = (me_j * num_i + me_i) * width + lax.broadcasted_iota(jnp.int32, (width, lanes), 0)
 
         def match(row, seen):
-            for inner in range(ids_ref.shape[2]):
+            for inner in range(ids_all.shape[3]):
                 names = ids_all[row // num_j, step_index, lax.rem(row, num_j), inner : inner + 1, :]
                 seen = jnp.where(names == stars, 1.0, seen)
             return seen
@@ -211,7 +211,7 @@
                     )
                 return sums
 
-            sums = lax.fori_loop(0, num_i, chunk, tuple(total_ref[row, rows, :] for row in range(6)))
+            sums = lax.fori_loop(0, num_i, chunk, tuple(total_ref[row, rows, :] for row in range(6)), unroll=True)
             for row in range(6):
                 total_ref[row, rows, :] = sums[row]
             return carry
@@ -231,8 +231,8 @@
         tall = jnp.concatenate(table, axis=0)
 
         def fill(owner, carry):
-            for row in range(ids_ref.shape[2]):
-                names = ids_ref[step_index, owner, row : row + 1, :]
+            for row in range(ids_all.shape[3]):
+                names = ids_all[me_i, step_index, owner, row : row + 1, :]
                 onehot = jnp.where(star == names, 1.0, 0.0).astype(jnp.bfloat16)
                 found = jnp.dot(tall, onehot, preferred_element_type=jnp.float32)
                 part[step_index, owner, :, row * lanes : (row + 1) * lanes] = found[0:8] + found[8:16] + found[16:24]
@@ -250,7 +250,16 @@
     barrier = pltpu.get_barrier_semaphore()
     for other in greeting:
         pl.semaphore_signal(barrier, inc=1, device_id=other, device_id_type=MESH)
-    ids_all[me_i] = ids_ref[...]
+    load = pltpu.make_async_copy(state_in, state_ref, load_sem)
+    load.start()
+    per_owner = ids_all.shape[3]
+    slot = lax.broadcasted_iota(jnp.int32, (1, lanes), 1)
+    for step_index in range(STEPS):
+        for row in range(raw_ref.shape[1]):
+            names = jnp.where(slot < counts_ref[step_index, row], raw_ref[step_index, row : row + 1, :], -1)
+            inner = row % per_owner
+            ids_all[me_i, step_index, row // per_owner, inner : inner + 1, :] = names
+    load.wait()
     mass_all = mass_ref[...]
     pos, vel = predict(state_ref[...], STEP_TIME + STEP_TIME * level_ref[...].astype(jnp.float32))
     for block in range(num_i):
@@ -290,7 +299,6 @@
     accumulate(field_next, me_j)
     for copy in column_force:
         copy.wait()
-    share(0, [rows_a[block] for block in range(num_i)])
     for copy, (_, owner) in zip(coming, along_j):
         copy.wait_recv()
         accumulate(field_next, owner)
@@ -300,6 +308,7 @@
     state = jnp.where(used, correct(state, force[0:3], force[3:6], span), state)
     rows_b[me_i] = jnp.concatenate([force, blank[:, :], state, blank, blank], axis=0)
     column = to_column(rows_b.at[me_i], sb, rb)
+    share(0, [rows_a[block] for block in range(num_i)])
     first_parts = send_parts(0, sq.at[0], rq.at[0])
     for copy in column:
         copy.wait()
@@ -322,19 +331,17 @@
     width = shard // num_i
     f32 = jnp.float32
     rows, lanes = active_ids.shape[1], active_ids.shape[2]
-    slot_pos = lax.broadcasted_iota(jnp.int32, active_ids.shape, 2)
-    ids = jnp.where(slot_pos < active_counts[:, :, None], active_ids, -1)
-    ids = ids.reshape(STEPS, num_j, rows // num_j, lanes)
     share = (rows // num_j) * lanes
     dma_j, dma_i = pltpu.SemaphoreType.DMA((num_j - 1,)), pltpu.SemaphoreType.DMA((num_i - 1,))
     dma_2 = pltpu.SemaphoreType.DMA((STEPS, num_j - 1))
     return pl.pallas_call(
         functools.partial(whole_kernel, sizes),
         out_shape=(jax.ShapeDtypeStruct((12, shard), f32), jax.ShapeDtypeStruct((STEPS, 6, share), f32)),
-        in_specs=[VMEM] * 4,
+        in_specs=[pl.BlockSpec(memory_space=pl.ANY), VMEM, VMEM, VMEM, pl.BlockSpec(memory_space=pltpu.SMEM)],
         out_specs=(VMEM,) * 2,
         scratch_shapes=[
-            pltpu.VMEM((num_i,) + ids.shape, jnp.int32),
+            pltpu.VMEM((12, shard), f32),
+            pltpu.VMEM((num_i, STEPS, num_j, rows // num_j, lanes), jnp.int32),
             pltpu.VMEM((num_j, num_i, 8, width), f32),
             pltpu.VMEM((num_j, num_i, 8, width), f32),
             pltpu.VMEM((num_i, 8, width), f32),
@@ -343,10 +350,10 @@
             pltpu.VMEM((STEPS, num_j, 8, share), f32),
             pltpu.VMEM((6, width, 128), f32),
             pltpu.VMEM((6, width, 128), f32),
-            dma_i, dma_i, dma_j, dma_j, dma_j, dma_j, dma_i, dma_i, dma_i, dma_i, dma_i, dma_i, dma_2, dma_2,
+            pltpu.SemaphoreType.DMA, dma_i, dma_i, dma_j, dma_j, dma_j, dma_j, dma_i, dma_i, dma_i, dma_i, dma_i, dma_i, dma_2, dma_2,
         ],
         compiler_params=pltpu.CompilerParams(collective_id=0, has_side_effects=True, vmem_limit_bytes=32 * 2**20),
-    )(phase_space, star_mass.reshape(1, shard), star_level.reshape(1, shard), ids)
+    )(phase_space, star_mass.reshape(1, shard), star_level.reshape(1, shard), active_ids, active_counts)
 
 
 def solution(mesh):

time: 61 us -> 53.9 us (0.88)
  Pallas kernels: 56.5 us -> 48.1 us
  local copies, waits for them, and re-layouts: 2.75 us -> 4.84 us
  other arithmetic: 0.81 us -> 0 us
    pallas_call x1, Pallas kernels: 56.5 us -> 48.1 us  [star_order(): pl.pallas_call(functools.partial(whole_kernel, sizes), out_shape=(jax.Sha...]
    unnamed x9 -> x11, local copies, waits for them, and re-layouts: 2.14 us -> 4.23 us
    select_n x1 -> x0, other arithmetic: 0.81 us -> none  [star_order(): ids = jnp.where(slot_pos < active_counts[:, :, None], active_ids, -1)]
where the time goes in v3:
time: 53.9 us; the launch traced here: 53.6 us
  Pallas kernels  48.1 us (89%)
  local copies, waits for them, and re-layouts  4.84 us (9%)
  between operations  0.65 us (1%)
    pallas_call x1, Pallas kernels, star_order(): pl.pallas_call(functools.partial(whole_kernel, sizes), out_shape=(jax.Sha...  48.1 us
    unnamed x11, local copies, waits for them, and re-layouts  4.23 us

profile of v3, /device:TPU:0, one launch (start us, length us, event | category | flops | bytes accessed | tf_op | source)
XLA Modules:
  0.0 53.6 jit_solution(15323973118879003781)
XLA Ops:
  0.6 0.0 copy-start.4
  0.6 0.7 %copy-done.4 = s32[2,16]{1,0:T(2,128)S(1)} copy-done((s32[2,16]{1,0:T(2,128)S(1)}, s32[2,16]{1,0:T(2,128)}, u32[]{:S(2)}) %copy-start.4) | copy-done | bytes 152
  1.3 0.0 copy-start
  1.3 0.8 %copy-done = f32[12,1024]{1,0:T(8,128)S(1)} copy-done((f32[12,1024]{1,0:T(8,128)S(1)}, f32[12,1024]{1,0:T(8,128)}, u32[]{:S(2)}) %copy-start) | copy-done | bytes 49176
  2.2 0.0 copy-start.1
  2.2 0.7 %copy-done.1 = s32[2,16,128]{2,1,0:T(8,128)S(1)} copy-done((s32[2,16,128]{2,1,0:T(8,128)S(1)}, s32[2,16,128]{2,1,0:T(8,128)}, u32[]{:S(2)}) %copy-start.1) | copy-done | bytes 16408
  2.9 0.0 copy-start.2
  2.9 0.7 %copy-done.2 = f32[1024]{0:T(1024)S(1)} copy-done((f32[1024]{0:T(1024)S(1)}, f32[1024]{0:T(1024)}, u32[]{:S(2)}) %copy-start.2) | copy-done | bytes 4120
  3.6 0.0 copy-start.3
  3.6 0.7 %copy-done.3 = s32[1024]{0:T(1024)S(1)} copy-done((s32[1024]{0:T(1024)S(1)}, s32[1024]{0:T(1024)}, u32[]{:S(2)}) %copy-start.3) | copy-done | bytes 4120
  4.2 48.1 %shard_map.68 = (f32[12,1024]{1,0:T(8,128)S(1)}, f32[2,6,256]{2,1,0:T(8,128)S(1)}) custom-call(f32[12,1024]{1,0:T(8,128)S(1)} %copy-done, f32[1,1024]{1,0:T(1,128)S(1)} %bitcast.2, s32[1,1024]{1,0:T(1,128)S(1)} %bitcast.3, s32[2,16,128]{2,1,0:T(8,128)S(1)} %copy-done.1, s32[2,16]{1,0:T(2,128)S(1)} %copy-done.4), custom_call_target="tpu_custom_call" | custom-call | tf_op jit(solution)/shard_map/pallas_call | solution.py:337
  52.3 0.6 %copy.7 = f32[2,6,256]{2,0,1:T(2,128)} copy(f32[2,6,256]{2,1,0:T(8,128)S(1)} %get-tuple-element.3) | data formatting | bytes 24576 | tf_op jit(solution)/shard_map/pallas_call | solution.py:337
  53.0 0.6 %copy.9 = f32[12,1024]{1,0:T(8,128)} copy(f32[12,1024]{1,0:T(8,128)S(1)} %get-tuple-element.6) | data formatting | bytes 98304
Async XLA Ops:
  0.6 0.7 %copy-start.4 = (s32[2,16]{1,0:T(2,128)S(1)}, s32[2,16]{1,0:T(2,128)}, u32[]{:S(2)}) copy-start(s32[2,16]{1,0:T(2,128)} %counts_ref.1) | copy-start | bytes 388
  1.3 0.8 %copy-start = (f32[12,1024]{1,0:T(8,128)S(1)}, f32[12,1024]{1,0:T(8,128)}, u32[]{:S(2)}) copy-start(f32[12,1024]{1,0:T(8,128)} %state_in.1) | copy-start | bytes 147460
  2.2 0.7 %copy-start.1 = (s32[2,16,128]{2,1,0:T(8,128)S(1)}, s32[2,16,128]{2,1,0:T(8,128)}, u32[]{:S(2)}) copy-start(s32[2,16,128]{2,1,0:T(8,128)} %raw_ref.1) | copy-start | bytes 49156
  2.9 0.7 %copy-start.2 = (f32[1024]{0:T(1024)S(1)}, f32[1024]{0:T(1024)}, u32[]{:S(2)}) copy-start(f32[1024]{0:T(1024)} %param.6) | copy-start | bytes 12292
  3.6 0.7 %copy-start.3 = (s32[1024]{0:T(1024)S(1)}, s32[1024]{0:T(1024)}, u32[]{:S(2)}) copy-start(s32[1024]{0:T(1024)} %param.7) | copy-start | bytes 12292

commit v4 on v3

--- a/solution.py
+++ b/solution.py
@@ -148,8 +148,8 @@
 
 
 def whole_kernel(
-    sizes, state_in, mass_ref, level_ref, raw_ref, counts_ref, out_ref, force_ref,
-    state_ref, ids_all, field, field_next, rows_a, rows_b, part, got, target_ref, total_ref,
+    sizes, state_in, mass_in, level_in, raw_in, counts_in, out_ref, force_ref,
+    state_ref, mass_ref, level_ref, raw_ref, counts_ref, ids_all, field, field_next, rows_a, rows_b, part, got, target_ref, total_ref,
     load_sem, sk, rk, sf, rf, sg, rg, sa, ra, sb, rb, sp, rp, sq, rq,
 ):
     num_i, num_j = sizes
@@ -246,12 +246,20 @@
             for n, (other, _) in enumerate(along_j)
         ]
 
+    loads = [
+        pltpu.make_async_copy(source, target, load_sem.at[n])
+        for n, (source, target) in enumerate((
+            (counts_in, counts_ref), (raw_in, raw_ref), (level_in, level_ref), (mass_in, mass_ref), (state_in, state_ref)
+        ))
+    ]
+    for copy in loads:
+        copy.start()
     greeting = [other for other, _ in along_j + along_i]
     barrier = pltpu.get_barrier_semaphore()
     for other in greeting:
         pl.semaphore_signal(barrier, inc=1, device_id=other, device_id_type=MESH)
-    load = pltpu.make_async_copy(state_in, state_ref, load_sem)
-    load.start()
+    for copy in loads:
+        copy.wait()
     per_owner = ids_all.shape[3]
     slot = lax.broadcasted_iota(jnp.int32, (1, lanes), 1)
     for step_index in range(STEPS):
@@ -259,7 +267,6 @@
             names = jnp.where(slot < counts_ref[step_index, row], raw_ref[step_index, row : row + 1, :], -1)
             inner = row % per_owner
             ids_all[me_i, step_index, row // per_owner, inner : inner + 1, :] = names
-    load.wait()
     mass_all = mass_ref[...]
     pos, vel = predict(state_ref[...], STEP_TIME + STEP_TIME * level_ref[...].astype(jnp.float32))
     for block in range(num_i):
@@ -337,10 +344,14 @@
     return pl.pallas_call(
         functools.partial(whole_kernel, sizes),
         out_shape=(jax.ShapeDtypeStruct((12, shard), f32), jax.ShapeDtypeStruct((STEPS, 6, share), f32)),
-        in_specs=[pl.BlockSpec(memory_space=pl.ANY), VMEM, VMEM, VMEM, pl.BlockSpec(memory_space=pltpu.SMEM)],
+        in_specs=[pl.BlockSpec(memory_space=pltpu.HBM)] * 5,
         out_specs=(VMEM,) * 2,
         scratch_shapes=[
             pltpu.VMEM((12, shard), f32),
+            pltpu.VMEM((1, shard), f32),
+            pltpu.VMEM((1, shard), jnp.int32),
+            pltpu.VMEM(active_ids.shape, jnp.int32),
+            pltpu.SMEM(active_counts.shape, jnp.int32),
             pltpu.VMEM((num_i, STEPS, num_j, rows // num_j, lanes), jnp.int32),
             pltpu.VMEM((num_j, num_i, 8, width), f32),
             pltpu.VMEM((num_j, num_i, 8, width), f32),
@@ -350,7 +361,7 @@
             pltpu.VMEM((STEPS, num_j, 8, share), f32),
             pltpu.VMEM((6, width, 128), f32),
             pltpu.VMEM((6, width, 128), f32),
-            pltpu.SemaphoreType.DMA, dma_i, dma_i, dma_j, dma_j, dma_j, dma_j, dma_i, dma_i, dma_i, dma_i, dma_i, dma_i, dma_2, dma_2,
+            pltpu.SemaphoreType.DMA((5,)), dma_i, dma_i, dma_j, dma_j, dma_j, dma_j, dma_i, dma_i, dma_i, dma_i, dma_i, dma_i, dma_2, dma_2,
         ],
         compiler_params=pltpu.CompilerParams(collective_id=0, has_side_effects=True, vmem_limit_bytes=32 * 2**20),
     )(phase_space, star_mass.reshape(1, shard), star_level.reshape(1, shard), active_ids, active_counts)

time: 53.9 us -> 54 us (level)
  no operation moved by 1% of the time
where the time goes in v4:
time: 54 us; the launch traced here: 53.6 us
  Pallas kernels  48.1 us (89%)
  local copies, waits for them, and re-layouts  4.84 us (9%)
  between operations  0.65 us (1%)
    pallas_call x1, Pallas kernels, star_order(): pl.pallas_call(functools.partial(whole_kernel, sizes), out_shape=(jax.Sha...  48.1 us
    unnamed x11, local copies, waits for them, and re-layouts  4.23 us

profile of v4, /device:TPU:0, one launch (start us, length us, event | category | flops | bytes accessed | tf_op | source)
XLA Modules:
  0.0 53.6 jit_solution(13900552603292535865)
XLA Ops:
  0.6 0.0 copy-start.4
  0.6 0.7 %copy-done.4 = s32[2,16]{1,0:T(2,128)S(1)} copy-done((s32[2,16]{1,0:T(2,128)S(1)}, s32[2,16]{1,0:T(2,128)}, u32[]{:S(2)}) %copy-start.4) | copy-done | bytes 152
  1.3 0.0 copy-start
  1.3 0.8 %copy-done = f32[12,1024]{1,0:T(8,128)S(1)} copy-done((f32[12,1024]{1,0:T(8,128)S(1)}, f32[12,1024]{1,0:T(8,128)}, u32[]{:S(2)}) %copy-start) | copy-done | bytes 49176
  2.2 0.0 copy-start.1
  2.2 0.7 %copy-done.1 = s32[2,16,128]{2,1,0:T(8,128)S(1)} copy-done((s32[2,16,128]{2,1,0:T(8,128)S(1)}, s32[2,16,128]{2,1,0:T(8,128)}, u32[]{:S(2)}) %copy-start.1) | copy-done | bytes 16408
  2.9 0.0 copy-start.2
  2.9 0.7 %copy-done.2 = f32[1024]{0:T(1024)S(1)} copy-done((f32[1024]{0:T(1024)S(1)}, f32[1024]{0:T(1024)}, u32[]{:S(2)}) %copy-start.2) | copy-done | bytes 4120
  3.6 0.0 copy-start.3
  3.6 0.7 %copy-done.3 = s32[1024]{0:T(1024)S(1)} copy-done((s32[1024]{0:T(1024)S(1)}, s32[1024]{0:T(1024)}, u32[]{:S(2)}) %copy-start.3) | copy-done | bytes 4120
  4.2 48.1 %shard_map.68 = (f32[12,1024]{1,0:T(8,128)S(1)}, f32[2,6,256]{2,1,0:T(8,128)S(1)}) custom-call(f32[12,1024]{1,0:T(8,128)S(1)} %copy-done, f32[1,1024]{1,0:T(1,128)S(1)} %bitcast.2, s32[1,1024]{1,0:T(1,128)S(1)} %bitcast.3, s32[2,16,128]{2,1,0:T(8,128)S(1)} %copy-done.1, s32[2,16]{1,0:T(2,128)S(1)} %copy-done.4), custom_call_target="tpu_custom_call" | custom-call | tf_op jit(solution)/shard_map/pallas_call | solution.py:344
  52.4 0.6 %copy.7 = f32[2,6,256]{2,0,1:T(2,128)} copy(f32[2,6,256]{2,1,0:T(8,128)S(1)} %get-tuple-element.3) | data formatting | bytes 24576 | tf_op jit(solution)/shard_map/pallas_call | solution.py:344
  53.0 0.6 %copy.9 = f32[12,1024]{1,0:T(8,128)} copy(f32[12,1024]{1,0:T(8,128)S(1)} %get-tuple-element.6) | data formatting | bytes 98304
Async XLA Ops:
  0.6 0.7 %copy-start.4 = (s32[2,16]{1,0:T(2,128)S(1)}, s32[2,16]{1,0:T(2,128)}, u32[]{:S(2)}) copy-start(s32[2,16]{1,0:T(2,128)} %counts_in.1) | copy-start | bytes 388
  1.3 0.8 %copy-start = (f32[12,1024]{1,0:T(8,128)S(1)}, f32[12,1024]{1,0:T(8,128)}, u32[]{:S(2)}) copy-start(f32[12,1024]{1,0:T(8,128)} %state_in.1) | copy-start | bytes 147460
  2.2 0.7 %copy-start.1 = (s32[2,16,128]{2,1,0:T(8,128)S(1)}, s32[2,16,128]{2,1,0:T(8,128)}, u32[]{:S(2)}) copy-start(s32[2,16,128]{2,1,0:T(8,128)} %raw_in.1) | copy-start | bytes 49156
  2.9 0.7 %copy-start.2 = (f32[1024]{0:T(1024)S(1)}, f32[1024]{0:T(1024)}, u32[]{:S(2)}) copy-start(f32[1024]{0:T(1024)} %param.6) | copy-start | bytes 12292
  3.6 0.7 %copy-start.3 = (s32[1024]{0:T(1024)S(1)}, s32[1024]{0:T(1024)}, u32[]{:S(2)}) copy-start(s32[1024]{0:T(1024)} %param.7) | copy-start | bytes 12292

commit v5 on v4

--- a/solution.py
+++ b/solution.py
@@ -363,7 +363,7 @@
             pltpu.VMEM((6, width, 128), f32),
             pltpu.SemaphoreType.DMA((5,)), dma_i, dma_i, dma_j, dma_j, dma_j, dma_j, dma_i, dma_i, dma_i, dma_i, dma_i, dma_i, dma_2, dma_2,
         ],
-        compiler_params=pltpu.CompilerParams(collective_id=0, has_side_effects=True, vmem_limit_bytes=32 * 2**20),
+        compiler_params=pltpu.CompilerParams(collective_id=0, has_side_effects=True, vmem_limit_bytes=63 * 2**20),
     )(phase_space, star_mass.reshape(1, shard), star_level.reshape(1, shard), active_ids, active_counts)
 
 

time: 54 us -> 52.4 us (0.970)
  local copies, waits for them, and re-layouts: 4.84 us -> 2.8 us
  Pallas kernels: 48.1 us -> 48.7 us
    unnamed x11 -> x1, local copies, waits for them, and re-layouts: 4.23 us -> 1.47 us
    pallas_call x1, local copies, waits for them, and re-layouts: 0.61 us -> 1.32 us  [star_order(): pl.pallas_call(functools.partial(whole_kernel, sizes), out_shape=(jax.Sha...]
    pallas_call x1, Pallas kernels: 48.1 us -> 48.7 us  [star_order(): pl.pallas_call(functools.partial(whole_kernel, sizes), out_shape=(jax.Sha...]
where the time goes in v5:
time: 52.4 us; the launch traced here: 52.2 us
  Pallas kernels  48.7 us (93%)
  local copies, waits for them, and re-layouts  2.8 us (5%)
  between operations  0.64 us (1%)
    pallas_call x1, Pallas kernels, star_order(): pl.pallas_call(functools.partial(whole_kernel, sizes), out_shape=(jax.Sha...  48.7 us
    unnamed x1, local copies, waits for them, and re-layouts  1.47 us
    pallas_call x1, local copies, waits for them, and re-layouts, star_order(): pl.pallas_call(functools.partial(whole_kernel, sizes), out_shape=(jax.Sha...  1.32 us

profile of v5, /device:TPU:0, one launch (start us, length us, event | category | flops | bytes accessed | tf_op | source)
XLA Modules:
  0.0 52.2 jit_solution(18126139015578361434)
XLA Ops:
  0.6 48.7 %shard_map.68 = (f32[12,1024]{1,0:T(8,128)}, f32[2,6,256]{2,1,0:T(8,128)}) custom-call(f32[12,1024]{1,0:T(8,128)} %state_in.1, f32[1,1024]{1,0:T(1,128)} %bitcast.2, s32[1,1024]{1,0:T(1,128)} %bitcast.3, s32[2,16,128]{2,1,0:T(8,128)} %raw_in.1, s32[2,16]{1,0:T(2,128)} %counts_in.1), custom_call_target="tpu_custom_call" | custom-call | tf_op jit(solution)/shard_map/pallas_call | solution.py:344
  49.4 1.3 %copy.7 = f32[2,6,256]{2,0,1:T(2,128)} copy(f32[2,6,256]{2,1,0:T(8,128)} %get-tuple-element.3) | data formatting | bytes 24576 | tf_op jit(solution)/shard_map/pallas_call | solution.py:344
  50.7 1.5 %copy.9 = f32[12,1024]{1,0:T(8,128)} copy(f32[12,1024]{1,0:T(8,128)} %get-tuple-element.6) | data formatting | bytes 98304

commit v6 on v4

--- a/solution.py
+++ b/solution.py
@@ -339,6 +339,7 @@
     f32 = jnp.float32
     rows, lanes = active_ids.shape[1], active_ids.shape[2]
     share = (rows // num_j) * lanes
+    operands = (phase_space, star_mass.reshape(1, shard), star_level.reshape(1, shard), active_ids, active_counts)
     dma_j, dma_i = pltpu.SemaphoreType.DMA((num_j - 1,)), pltpu.SemaphoreType.DMA((num_i - 1,))
     dma_2 = pltpu.SemaphoreType.DMA((STEPS, num_j - 1))
     return pl.pallas_call(
@@ -364,7 +365,7 @@
             pltpu.SemaphoreType.DMA((5,)), dma_i, dma_i, dma_j, dma_j, dma_j, dma_j, dma_i, dma_i, dma_i, dma_i, dma_i, dma_i, dma_2, dma_2,
         ],
         compiler_params=pltpu.CompilerParams(collective_id=0, has_side_effects=True, vmem_limit_bytes=32 * 2**20),
-    )(phase_space, star_mass.reshape(1, shard), star_level.reshape(1, shard), active_ids, active_counts)
+    )(*[pltpu.with_memory_space_constraint(array, pltpu.HBM) for array in operands])
 
 
 def solution(mesh):

time: 54 us -> 50.2 us (0.930)
  local copies, waits for them, and re-layouts: 4.84 us -> 1.24 us
    unnamed x11 -> x1, local copies, waits for them, and re-layouts: 4.23 us -> 0.63 us
where the time goes in v6:
time: 50.2 us; the launch traced here: 50 us
  Pallas kernels  48.1 us (96%)
  local copies, waits for them, and re-layouts  1.24 us (2%)
  between operations  0.64 us (1%)
    pallas_call x1, Pallas kernels, star_order(): pl.pallas_call(functools.partial(whole_kernel, sizes), out_shape=(jax.Sha...  48.1 us

profile of v6, /device:TPU:0, one launch (start us, length us, event | category | flops | bytes accessed | tf_op | source)
XLA Modules:
  0.0 50.0 jit_solution(3087395014331357636)
XLA Ops:
  0.6 48.1 %shard_map.68 = (f32[12,1024]{1,0:T(8,128)S(1)}, f32[2,6,256]{2,1,0:T(8,128)S(1)}) custom-call(f32[12,1024]{1,0:T(8,128)} %state_in.1, f32[1,1024]{1,0:T(1,128)} %bitcast.2, s32[1,1024]{1,0:T(1,128)} %bitcast.3, s32[2,16,128]{2,1,0:T(8,128)} %raw_in.1, s32[2,16]{1,0:T(2,128)} %counts_in.1), custom_call_target="tpu_custom_call" | custom-call | tf_op jit(solution)/shard_map/pallas_call | solution.py:345
  48.8 0.6 %copy.7 = f32[2,6,256]{2,0,1:T(2,128)} copy(f32[2,6,256]{2,1,0:T(8,128)S(1)} %get-tuple-element.3) | data formatting | bytes 24576 | tf_op jit(solution)/shard_map/pallas_call | solution.py:345
  49.4 0.6 %copy.9 = f32[12,1024]{1,0:T(8,128)} copy(f32[12,1024]{1,0:T(8,128)S(1)} %get-tuple-element.6) | data formatting | bytes 98304

commit v7 on v6

--- a/solution.py
+++ b/solution.py
@@ -184,12 +184,13 @@
             target_ref[row] = jnp.broadcast_to(columns[:, row : row + 1], (width, lanes))
         total_ref[...] = jnp.zeros_like(total_ref)
 
-    def accumulate(source, owner):
+    def accumulate(source, owner, start=0, stop=num_i, turn=0):
         def tile(index, carry):
             rows = pl.ds(pl.multiple_of(index * TILE, TILE), TILE)
             tx, ty, tz, tu, tv, tw = [target_ref[row, rows, :] for row in range(6)]
 
-            def chunk(block, sums):
+            def chunk(count, sums):
+                block = lax.rem(count + turn, num_i)
                 for first in range(0, width, lanes):
                     sx, sy, sz, su, sv, sw, mass = [
                         source[owner, block, row : row + 1, first : first + lanes] for row in range(7)
@@ -211,7 +212,7 @@
                     )
                 return sums
 
-            sums = lax.fori_loop(0, num_i, chunk, tuple(total_ref[row, rows, :] for row in range(6)), unroll=True)
+            sums = lax.fori_loop(start, stop, chunk, tuple(total_ref[row, rows, :] for row in range(6)), unroll=True)
             for row in range(6):
                 total_ref[row, rows, :] = sums[row]
             return carry
@@ -300,10 +301,11 @@
     column_force = to_column(rows_a.at[me_i], sp, rp)
     set_targets(field_next[me_j, me_i])
     used = used_row(1)
+    accumulate(field_next, me_j, 0, 1, me_i)
     for copy in column:
         copy.wait()
     coming = to_row(field_next.at[me_j], sg, rg)
-    accumulate(field_next, me_j)
+    accumulate(field_next, me_j, 1, num_i, me_i)
     for copy in column_force:
         copy.wait()
     for copy, (_, owner) in zip(coming, along_j):

time: 50.2 us -> 50.2 us (level)
  no operation moved by 1% of the time
where the time goes in v7:
time: 50.2 us; the launch traced here: 50 us
  Pallas kernels  48.1 us (96%)
  local copies, waits for them, and re-layouts  1.24 us (2%)
  between operations  0.64 us (1%)
    pallas_call x1, Pallas kernels, star_order(): pl.pallas_call(functools.partial(whole_kernel, sizes), out_shape=(jax.Sha...  48.1 us

profile of v7, /device:TPU:0, one launch (start us, length us, event | category | flops | bytes accessed | tf_op | source)
XLA Modules:
  0.0 50.0 jit_solution(9637118304122832681)
XLA Ops:
  0.6 48.1 %shard_map.68 = (f32[12,1024]{1,0:T(8,128)S(1)}, f32[2,6,256]{2,1,0:T(8,128)S(1)}) custom-call(f32[12,1024]{1,0:T(8,128)} %state_in.1, f32[1,1024]{1,0:T(1,128)} %bitcast.2, s32[1,1024]{1,0:T(1,128)} %bitcast.3, s32[2,16,128]{2,1,0:T(8,128)} %raw_in.1, s32[2,16]{1,0:T(2,128)} %counts_in.1), custom_call_target="tpu_custom_call" | custom-call | tf_op jit(solution)/shard_map/pallas_call | solution.py:347
  48.8 0.6 %copy.7 = f32[2,6,256]{2,0,1:T(2,128)} copy(f32[2,6,256]{2,1,0:T(8,128)S(1)} %get-tuple-element.3) | data formatting | bytes 24576 | tf_op jit(solution)/shard_map/pallas_call | solution.py:347
  49.4 0.6 %copy.9 = f32[12,1024]{1,0:T(8,128)} copy(f32[12,1024]{1,0:T(8,128)S(1)} %get-tuple-element.6) | data formatting | bytes 98304
